TPU v7x, 32 devices: a whole 2x2x4 slice. The times are simulated.
32 devices in a mesh: lat: 4 (over x, core), lon: 8 (over z, y).
Axes of the slice: x: 2, y: 2, z: 4, core: 2. Of those that a mesh axis runs over, the one named last changes fastest.
Arguments:
- adjoint_in: float32 [16, 3, 136, 1024], P('lat', None, None, 'lon'), may hold values from -6 to 6
- frac_x: float32 [16, 1024], P('lat', 'lon'), may hold values from 0 to 1
- frac_y: float32 [16, 1024], P('lat', 'lon'), may hold values from 0 to 1
- dep_tile: int32 [16], P('lat'), may hold values from -1 to 0, as said below
- dep_col: int32 [16], P('lat'), may hold values from 0 to 127
- block_inverse: float32 [16, 2, 68, 68], P('lat'), may hold values from -0.25 to 1
- coupling: float32 [16, 1024], P('lat', 'lon'), may hold values from 0.15 to 0.6
Outputs:
- adjoint_out: float32 [16, 3, 136, 1024], P('lat', None, None, 'lon')
Inputs may be any that keep to these rules, and one draw needn't show every extreme that they name: dep_tile * 128 + dep_col is the row's departure offset in columns; it equals -128 in some row and 127 in another.
All inputs are finite; a program needn't handle non-finite values.
Results may differ from a plain program's by a relative error of at most 0.0003.
Values sent between devices are 32-bit elements; how exact they have to be, the bound alone decides.
No kernel may reach another device: no remote copies, remote signals or barrier semaphores. Data moves between devices by JAX's collectives and lax.ppermute only.
A program may use at most 64 MiB of HBM per device.

v0:
```python
import jax
import jax.numpy as jnp
from jax import lax
from jax.sharding import PartitionSpec as P

REACH = 1


def passed_along(x, axis, by):
    devices = lax.axis_size(axis)
    return lax.ppermute(x, axis, [(i, (i + by) % devices) for i in range(devices)])


def shifted(x, axis, by):
    devices = lax.axis_size(axis)
    pairs = [(i, i + by) for i in range(devices) if 0 <= i + by < devices]
    return lax.ppermute(x, axis, pairs)


def cubic_weights(fraction):
    plus_one = fraction + 1.0
    minus_one = fraction - 1.0
    minus_two = fraction - 2.0
    return jnp.stack(
        [
            -fraction * minus_one * minus_two / 6.0,
            plus_one * minus_one * minus_two / 2.0,
            -plus_one * fraction * minus_two / 2.0,
            plus_one * fraction * minus_one / 6.0,
        ]
    )


def vertical(field_in, inverse, coupling):
    row_count, tracer_count, level_count, col_count = field_in.shape
    block_count = inverse.shape[1]
    block_size = inverse.shape[2]
    blocks = field_in.reshape(row_count, tracer_count, block_count, block_size, col_count)
    first_sweep = jnp.einsum("rnij,rtnjc->rtnic", inverse, blocks, precision=lax.Precision.HIGHEST)
    coupling_now = coupling[:, None, None, :]
    adjusted = blocks.at[:, :, :-1, block_size - 1, :].add(
        coupling_now * first_sweep[:, :, 1:, 0, :]
    )
    adjusted = adjusted.at[:, :, 1:, 0, :].add(
        coupling_now * first_sweep[:, :, :-1, block_size - 1, :]
    )
    second_sweep = jnp.einsum(
        "rnij,rtnjc->rtnic", inverse, adjusted, precision=lax.Precision.HIGHEST
    )
    return second_sweep.reshape(row_count, tracer_count, level_count, col_count)


def prepare(values, frac_x, frac_y):
    weights_x = jnp.swapaxes(cubic_weights(frac_x), 0, 1)
    weights_y = jnp.swapaxes(cubic_weights(frac_y), 0, 1)
    paired = weights_y[:, :, None, :] * weights_x[:, None, :, :]
    zero_block = jnp.zeros(values.shape, jnp.float32)
    zero_pairs = jnp.zeros(paired.shape, jnp.float32)
    padded_values = jnp.concatenate([zero_block, values, zero_block], axis=3)
    padded_pairs = jnp.concatenate([zero_pairs, paired, zero_pairs], axis=3)
    return (padded_values, padded_pairs)


def tile_terms(padded_values, padded_pairs, offsets, k, col_count):
    row_count = padded_values.shape[0]

    def one_row(packed):
        row_values, row_pairs, offset = packed
        summed = None
        for b in range(4):
            delta = k * col_count + 1 - b - offset
            reached = (jnp.abs(delta) < col_count).astype(jnp.float32)
            start = jnp.clip(col_count + delta, 0, 2 * col_count)
            sliced = lax.dynamic_slice_in_dim(row_values, start, col_count, 2)
            factor = lax.dynamic_slice_in_dim(row_pairs[:, b, :], start, col_count, 1) * reached
            product_term = factor[:, None, None, :] * sliced[None]
            summed = product_term if b == 0 else summed + product_term
        return summed

    summed = lax.map(one_row, (padded_values, padded_pairs, offsets))
    extended = jnp.zeros((row_count + 3,) + summed.shape[2:], jnp.float32)
    for a in range(4):
        extended = extended.at[a : a + row_count].add(summed[:, a])
    return extended


def on_device(adjoint_in, frac_x, frac_y, dep_tile, dep_col, block_inverse, coupling):
    row_count = adjoint_in.shape[0]
    col_count = adjoint_in.shape[3]
    offsets = dep_tile * col_count + dep_col
    far_tiles = REACH + 1
    padded_values, padded_pairs = prepare(adjoint_in, frac_x, frac_y)
    home_sum = tile_terms(padded_values, padded_pairs, offsets, 0, col_count)
    for k in range(-far_tiles, far_tiles + 1):
        if k != 0:
            outgoing = tile_terms(padded_values, padded_pairs, offsets, k, col_count)
            home_sum = home_sum + passed_along(outgoing, "lon", k)
    upper_rim = shifted(home_sum[row_count + 1 : row_count + 3], "lat", 1)
    lower_rim = shifted(home_sum[0:1], "lat", -1)
    interior = home_sum[1 : row_count + 1]
    interior = interior.at[0:2].add(upper_rim)
    interior = interior.at[row_count - 1 : row_count].add(lower_rim)
    return vertical(interior, block_inverse, coupling)


def solution(mesh):
    return jax.shard_map(
        on_device,
        mesh=mesh,
        in_specs=(
            P("lat", None, None, "lon"),
            P("lat", "lon"),
            P("lat", "lon"),
            P("lat"),
            P("lat"),
            P("lat", None, None, None),
            P("lat", "lon"),
        ),
        out_specs=P("lat", None, None, "lon"),
        check_vma=False,
    )
```

profile of v0, /device:TPU:1, one launch (start us, length us, event | category | flops | bytes accessed | tf_op | source)
XLA Modules:
  0.0 228.0 jit_solution(15496796711692372386)
XLA Ops:
  1.6 1.3 pad_maximum_fusion
  3.0 1.9 broadcast.990.clone2.3
  4.9 29.5 %while.90 = (s32[]{:T(128)}, f32[4,4,3,136,128]{4,3,2,0,1:T(8,128)}, f32[4,4,4,384]{3,1,2,0:T(4,128)S(1)}, s32[4]{0:T(128)S(1)}, f32[4,3,136,384]{3,2,1,0:T(8,12...) while((s32[]{:T(128)}, ...), condition=%wide.region_3.4_spmd, body=%wide.region_2.3_spmd.sunk | while | flops 1464355 | bytes 3466337 | solution.py:80
  11.2 1.1 bitcast_dynamic-update-slice_fusion.9
  33.3 1.1 bitcast_dynamic-update-slice_fusion.9
  34.4 1.4 slice_bitcast_fusion.5
  35.8 1.2 scatter-add.86
  37.0 2.1 fusion.55
  39.1 2.1 fusion.50
  41.3 2.2 fusion.49
  43.5 4.2 %collective-permute-start = (f32[7,3,136,128]{3,2,1,0:T(8,128)}, f32[7,3,136,128]{3,2,1,0:T(8,128)}, u32[]{:S(2)}, u32[]{:S(2)}) collective-permute-start(f32[7,3,136,128]{3,2,1,0:T(8,128)} %fusion.49), channel_id=1, source_target_pairs={{0,6},{1,7},{2,0},{3,1},{4,2},{5,3},{6,4},{7,5},{8,14},{9,15},{10,... | collective-permute-start | bytes 4386824 | tf_op jit(solution)/shard_map/ppermute | solution.py:11
  47.6 1.9 broadcast.990.clone2.1
  49.5 29.1 %while.91 = (s32[]{:T(128)}, f32[4,4,3,136,128]{4,3,2,0,1:T(8,128)}, f32[4,4,4,384]{3,1,2,0:T(4,128)S(1)}, s32[4]{0:T(128)S(1)}, f32[4,3,136,384]{3,2,1,0:T(8,12...) while((s32[]{:T(128)}, ...), condition=%wide.region_5.6_spmd, body=%wide.region_4.5_spmd.sunk | while | flops 1464355 | bytes 3466329 | solution.py:80
  55.7 1.1 bitcast_dynamic-update-slice_fusion.10
  77.5 1.1 bitcast_dynamic-update-slice_fusion.10
  78.7 1.4 slice_bitcast_fusion.4
  80.0 1.2 scatter-add.94
  81.2 2.2 fusion.54
  83.4 2.1 fusion.48
  85.5 2.1 fusion.47
  87.7 1.1 collective-permute-start.1
  88.8 1.9 broadcast.990.clone2
  90.7 29.5 %while.92 = (s32[]{:T(128)}, f32[4,4,3,136,128]{4,3,2,0,1:T(8,128)}, f32[4,4,4,384]{3,1,2,0:T(4,128)S(1)}, s32[4]{0:T(128)S(1)}, f32[4,3,136,384]{3,2,1,0:T(8,12...) while((s32[]{:T(128)}, ...), condition=%wide.region_7.8_spmd, body=%wide.region_6.7_spmd.sunk | while | flops 1464355 | bytes 3466321 | solution.py:80
  97.0 1.1 bitcast_dynamic-update-slice_fusion.11
  119.1 1.1 bitcast_dynamic-update-slice_fusion.11
  120.2 1.4 slice_bitcast_fusion.3
  121.6 1.2 scatter-add.100
  122.8 2.1 fusion.53
  124.9 2.1 fusion.46
  127.1 2.1 fusion.45
  129.6 29.2 %while.93 = (s32[]{:T(128)}, f32[4,4,3,136,128]{4,3,2,1,0:T(8,128)}, f32[4,4,4,384]{3,1,2,0:T(4,128)S(1)}, s32[4]{0:T(128)S(1)}, f32[4,3,136,384]{3,2,1,0:T(8,12...) while((s32[]{:T(128)}, ...), condition=%wide.region_9.10_spmd, body=%wide.region_8.9_spmd.sunk | while | flops 1464355 | bytes 3466329 | solution.py:80
  143.1 1.1 add_dynamic-update-slice_fusion.2
  158.8 1.4 slice_bitcast_fusion.2
  160.1 1.2 scatter-add.106
  161.3 2.2 fusion.44
  163.5 2.1 fusion.42
  165.6 2.1 fusion.40
  168.7 1.9 broadcast.990.clone2.2
  170.7 29.5 %while.89 = (s32[]{:T(128)}, f32[4,4,3,136,128]{4,3,2,0,1:T(8,128)}, f32[4,4,4,384]{3,1,2,0:T(4,128)S(1)}, s32[4]{0:T(128)S(1)}, f32[4,3,136,384]{3,2,1,0:T(8,12...) while((s32[]{:T(128)}, ...), condition=%wide.region_1.2_spmd, body=%wide.region_0.1_spmd.sunk | while | flops 1464355 | bytes 3466321 | solution.py:80
  199.0 1.1 bitcast_dynamic-update-slice_fusion.8
  200.2 1.4 slice_bitcast_fusion.6
  202.9 3.0 %add_add_fusion = f32[7,3,136,128]{3,2,1,0:T(8,128)S(1)} fusion(f32[7,3,136,128]{3,2,1,0:T(8,128)} %collective-permute-done.3, f32[7,3,136,128]{3,2,1,0:T(8,128)} %collective-permute-done.2, f32[7,3,136,128]{3,2,1,0:T(8,128)} %collective-permute-done.1, f32[7,3,136,128]{3,2,1,0:T(8,128)S(1)} %fusion.51, f32[7,3,136,128]{3,2,1,0:T(8,128)} %collective-permute-done), kind=kLoop, calls=%fused_computation.91 | loop fusion | flops 1462272 | bytes 8773632 | tf_op jit(solution)/shard_map/add | solution.py:97
  205.9 4.5 %collective-permute-start.4 = (f32[2,3,136,128]{3,2,1,0:T(8,128)S(1)}, f32[2,3,136,128]{3,2,1,0:T(8,128)S(1)}, u32[]{:S(2)}, u32[]{:S(2)}) collective-permute-start(f32[2,3,136,128]{3,2,1,0:T(8,128)S(1)} %slice.996), channel_id=1, source_target_pairs={{0,8},{8,16},{16,24},{1,9},{9,17},{17,25},{2,10},{10,18},{18,26},{... | collective-permute-start | bytes 1253384 | tf_op jit(solution)/shard_map/ppermute | solution.py:17
  211.9 1.9 collective-permute-start.5
  213.9 1.6 collective-permute-done.4
  215.5 3.6 %collective-permute-done.5 = f32[1,3,136,128]{3,2,1,0:T(8,128)S(1)} collective-permute-done((f32[1,3,136,128]{3,2,1,0:T(8,128)S(1)}, f32[1,3,136,128]{3,2,1,0:T(8,128)S(1)}, u32[]{:S(2)}, u32[]{:S(2)}) %collective-permute-start.5) | collective-permute-done | bytes 208928 | tf_op jit(solution)/shard_map/ppermute | solution.py:17
  221.5 1.9 broadcast_select_fusion
  223.4 1.3 scatter-add.116
  (192 shorter events, 46.8 us)
Async XLA Ops:
  0.0 219.4 %copy-start = (f32[4,2,68,68]{3,1,2,0:T(2,128)S(1)}, f32[4,2,68,68]{3,1,2,0:T(2,128)}, u32[]{:S(2)}) copy-start(f32[4,2,68,68]{3,1,2,0:T(2,128)} %param.70) | copy-start | bytes 443908
  1.5 1.4 copy-start.9
  1.5 1.4 copy-start.10
  34.4 2.6 %copy-start.1 = (f32[4,4,3,136,128]{4,3,2,0,1:T(8,128)S(1)}, f32[4,4,3,136,128]{4,3,2,0,1:T(8,128)}, u32[]{:S(2)}) copy-start(f32[4,4,3,136,128]{4,3,2,0,1:T(8,128)} %get-tuple-element.784) | copy-start | bytes 10027012
  43.5 159.4 %collective-permute-start = (f32[7,3,136,128]{3,2,1,0:T(8,128)}, f32[7,3,136,128]{3,2,1,0:T(8,128)}, u32[]{:S(2)}, u32[]{:S(2)}) collective-permute-start(f32[7,3,136,128]{3,2,1,0:T(8,128)} %fusion.49), channel_id=1, source_target_pairs={{0,6},{1,7},{2,0},{3,1},{4,2},{5,3},{6,4},{7,5},{8,14},{9,15},{10,... | collective-permute-start | bytes 4386824 | tf_op jit(solution)/shard_map/ppermute | solution.py:11
  78.7 2.6 %copy-start.2 = (f32[4,4,3,136,128]{4,3,2,0,1:T(8,128)S(1)}, f32[4,4,3,136,128]{4,3,2,0,1:T(8,128)}, u32[]{:S(2)}) copy-start(f32[4,4,3,136,128]{4,3,2,0,1:T(8,128)} %get-tuple-element.785) | copy-start | bytes 10027012
  87.7 115.2 %collective-permute-start.1 = (f32[7,3,136,128]{3,2,1,0:T(8,128)}, f32[7,3,136,128]{3,2,1,0:T(8,128)}, u32[]{:S(2)}, u32[]{:S(2)}) collective-permute-start(f32[7,3,136,128]{3,2,1,0:T(8,128)} %fusion.47), channel_id=1, source_target_pairs={{0,7},{1,0},{2,1},{3,2},{4,3},{5,4},{6,5},{7,6},{8,15},{9,8},{10,9... | collective-permute-start | bytes 4386824 | tf_op jit(solution)/shard_map/ppermute | solution.py:11
  120.2 2.6 %copy-start.3 = (f32[4,4,3,136,128]{4,3,2,0,1:T(8,128)S(1)}, f32[4,4,3,136,128]{4,3,2,0,1:T(8,128)}, u32[]{:S(2)}) copy-start(f32[4,4,3,136,128]{4,3,2,0,1:T(8,128)} %get-tuple-element.786) | copy-start | bytes 10027012
  129.2 73.6 %collective-permute-start.2 = (f32[7,3,136,128]{3,2,1,0:T(8,128)}, f32[7,3,136,128]{3,2,1,0:T(8,128)}, u32[]{:S(2)}, u32[]{:S(2)}) collective-permute-start(f32[7,3,136,128]{3,2,1,0:T(8,128)} %fusion.45), channel_id=1, source_target_pairs={{0,1},{1,2},{2,3},{3,4},{4,5},{5,6},{6,7},{7,0},{8,9},{9,10},{10,1... | collective-permute-start | bytes 4386824 | tf_op jit(solution)/shard_map/ppermute | solution.py:11
  158.8 2.6 %copy-start.5 = (f32[4,4,3,136,128]{4,3,2,1,0:T(8,128)S(1)}, f32[4,4,3,136,128]{4,3,2,1,0:T(8,128)}, u32[]{:S(2)}) copy-start(f32[4,4,3,136,128]{4,3,2,1,0:T(8,128)} %get-tuple-element.787) | copy-start | bytes 10027012
  167.8 35.1 %collective-permute-start.3 = (f32[7,3,136,128]{3,2,1,0:T(8,128)}, f32[7,3,136,128]{3,2,1,0:T(8,128)}, u32[]{:S(2)}, u32[]{:S(2)}) collective-permute-start(f32[7,3,136,128]{3,2,1,0:T(8,128)} %fusion.40), channel_id=1, source_target_pairs={{0,2},{1,3},{2,4},{3,5},{4,6},{5,7},{6,0},{7,1},{8,10},{9,11},{10,... | collective-permute-start | bytes 4386824 | tf_op jit(solution)/shard_map/ppermute | solution.py:11
  200.1 2.2 copy-start.4
  202.8 8.3 %copy-start.8 = (s32[5]{0:T(128)S(1)}, s32[5]{0:T(128)}, u32[]{:S(2)}) copy-start(s32[5]{0:T(128)} %constant.1777.clone.1) | copy-start | bytes 64
  205.9 9.5 %collective-permute-start.4 = (f32[2,3,136,128]{3,2,1,0:T(8,128)S(1)}, f32[2,3,136,128]{3,2,1,0:T(8,128)S(1)}, u32[]{:S(2)}, u32[]{:S(2)}) collective-permute-start(f32[2,3,136,128]{3,2,1,0:T(8,128)S(1)} %slice.996), channel_id=1, source_target_pairs={{0,8},{8,16},{16,24},{1,9},{9,17},{17,25},{2,10},{10,18},{18,26},{... | collective-permute-start | bytes 1253384 | tf_op jit(solution)/shard_map/ppermute | solution.py:17
  211.9 7.1 %collective-permute-start.5 = (f32[1,3,136,128]{3,2,1,0:T(8,128)S(1)}, f32[1,3,136,128]{3,2,1,0:T(8,128)S(1)}, u32[]{:S(2)}, u32[]{:S(2)}) collective-permute-start(f32[1,3,136,128]{3,2,1,0:T(8,128)S(1)} %slice.998), channel_id=1, source_target_pairs={{8,0},{16,8},{24,16},{9,1},{17,9},{25,17},{10,2},{18,10},{26,18},{... | collective-permute-start | bytes 626696 | tf_op jit(solution)/shard_map/ppermute | solution.py:17
  219.1 2.4 %copy-start.7 = (f32[4,128]{1,0:T(4,128)S(1)}, f32[4,128]{1,0:T(4,128)}, u32[]{:S(2)}) copy-start(f32[4,128]{1,0:T(4,128)} %param.71) | copy-start | bytes 6148
  220.5 0.9 copy-start.6
where the time goes:
time: 230 us; the launch traced here: 228 us
  loops' own time  102 us (44%)
  other arithmetic  61.2 us (27%)
  local copies, waits for them, and re-layouts  43.8 us (19%)
  starting transfers between devices  13 us (6%)
  waiting for transfers between devices  5.16 us (2%)
    another operation x5, loops' own time, tile_terms(): summed = lax.map(one_row, (padded_values, padded_pairs, offsets))  102 us
    scatter-add x15, other arithmetic, tile_terms(): extended = extended.at[a:a + row_count].add(summed[:, a])  26.2 us
    dynamic_update_slice x20, other arithmetic, tile_terms(): summed = lax.map(one_row, (padded_values, padded_pairs, offsets))  22.3 us
    dynamic_slice x20, local copies, waits for them, and re-layouts, tile_terms(): summed = lax.map(one_row, (padded_values, padded_pairs, offsets))  12.5 us
    another operation x5, local copies, waits for them, and re-layouts  8.38 us
    add x5, local copies, waits for them, and re-layouts, tile_terms(): extended = extended.at[a:a + row_count].add(summed[:, a])  6.77 us
    ppermute x4, starting transfers between devices, passed_along(): lax.ppermute(x, axis, [(i, (i + by) % devices) for i in range(devices)])  6.58 us
    ppermute x2, starting transfers between devices, shifted(): return lax.ppermute(x, axis, pairs)  6.44 us
  transfers between devices with their start and end apart: 6, of which 2 were waited for; matrix products, arithmetic and copies ran while one was open for 31% of the time, Pallas kernels for 0%

commit v1 on v0

v1 whole, which is shorter than its diff:
```python
import functools

import jax
import jax.numpy as jnp
from jax import lax
from jax.experimental import pallas as pl
from jax.experimental.pallas import tpu as pltpu
from jax.sharding import PartitionSpec as P

PIECE = 8
VMEM_BYTES = 48 * 1024 * 1024


def passed_along(x, axis, by):
    devices = lax.axis_size(axis)
    return lax.ppermute(x, axis, [(i, (i + by) % devices) for i in range(devices)])


def shifted(x, axis, by):
    devices = lax.axis_size(axis)
    pairs = [(i, i + by) for i in range(devices) if 0 <= i + by < devices]
    return lax.ppermute(x, axis, pairs)


def wx_weights(f):
    return [
        -f * (f - 1.0) * (f - 2.0) / 6.0,
        (f + 1.0) * (f - 1.0) * (f - 2.0) / 2.0,
        -(f + 1.0) * f * (f - 2.0) / 2.0,
        (f + 1.0) * f * (f - 1.0) / 6.0,
    ]


def plan(tile_ref, col_ref, cols):
    rows = tile_ref.shape[0]
    right_at, left_at = jnp.int32(0), jnp.int32(0)
    entries = []
    for i in range(rows):
        s = tile_ref[i] * cols + col_ref[i]
        right_w = jnp.where(s >= 0, jnp.minimum(s + 2, cols), jnp.where(s == -1, 1, 0))
        left_w = jnp.where(s < 0, jnp.minimum(1 - s, cols), jnp.where(s == 0, 1, 0))
        entries.append((s, right_at, right_w, left_at, left_w))
        right_at = right_at + right_w
        left_at = left_at + left_w
    return entries, right_at, left_at


def pack_kernel(tile_ref, col_ref, x_ref, fx_ref, fy_ref, right_ref, left_ref, far_right_ref, far_left_ref, index_ref, even_ref, odd_ref):
    rows, levels, cols = x_ref.shape
    half = right_ref.shape[1]
    unit = cols // 2
    unit_count = right_ref.shape[0]
    entries, right_total, left_total = plan(tile_ref, col_ref, cols)
    index_ref[0] = ((right_total + unit - 1) // unit) * (unit_count + 1) + (left_total + unit - 1) // unit
    lane = lax.broadcasted_iota(jnp.int32, (half, cols), 1)
    sub8 = lax.broadcasted_iota(jnp.int32, (PIECE, cols), 0)

    for i in range(rows):
        s, right_at, right_w, left_at, left_w = entries[i]

        def lo_hi():
            lo = x_ref[i, 0:half, :]
            tail = jnp.where(sub8 == 0, fx_ref[i : i + 1, :], fy_ref[i : i + 1, :])
            hi = jnp.concatenate([x_ref[i, half:levels, :], tail], axis=0)
            return lo, hi

        def place(dst_ref, first, at, width):
            lo, hi = lo_hi()
            shift = jnp.bitwise_and(at - first, cols - 1)
            lo = pltpu.roll(lo, shift, 1)
            hi = pltpu.roll(hi, shift, 1)
            even_ref[...] = jnp.where(lane < unit, lo, pltpu.roll(hi, unit, 1))
            odd_ref[...] = jnp.where(lane < unit, pltpu.roll(lo, unit, 1), hi)
            window = at // cols
            for k in range(4):
                u = 2 * window + k
                src_ref = even_ref if k % 2 == 0 else odd_ref

                @pl.when((u * unit < at + width) & (u * unit + unit > at))
                def _():
                    uu = jnp.minimum(u, unit_count - 1)
                    place_of = uu * unit + jnp.bitwise_and(lane, unit - 1)
                    mask = (place_of >= at) & (place_of < at + width)
                    dst_ref[uu] = jnp.where(mask, src_ref[...], dst_ref[uu])

        @pl.when(right_w > 0)
        def _():
            place(right_ref, cols - right_w, right_at, right_w)

        @pl.when(left_w > 0)
        def _():
            place(left_ref, jnp.int32(0), left_at, left_w)

        def place_one(dst_ref, column):
            lo, hi = lo_hi()
            lo = pltpu.roll(lo, (i - column) % cols, 1)
            hi = pltpu.roll(hi, (unit + i - column) % cols, 1)
            dst_ref[...] = jnp.where(lane == i, lo, jnp.where(lane == unit + i, hi, dst_ref[...]))

        @pl.when(s == cols - 1)
        def _():
            place_one(far_right_ref, cols - 1)

        @pl.when(s == -cols)
        def _():
            place_one(far_left_ref, 0)


def spread_kernel(tile_ref, col_ref, x_ref, fx_ref, fy_ref, right_ref, left_ref, far_right_ref, far_left_ref, down_ref, mid_ref, up_ref, lo_ref, hi_ref, weight_ref):
    rows, levels, cols = x_ref.shape
    half = right_ref.shape[1]
    unit = cols // 2
    unit_count = right_ref.shape[0]
    entries, _, _ = plan(tile_ref, col_ref, cols)
    lane = lax.broadcasted_iota(jnp.int32, (PIECE, cols), 1)
    lane_big = lax.broadcasted_iota(jnp.int32, (half, cols), 1)
    sub8 = lax.broadcasted_iota(jnp.int32, (PIECE, cols), 0)

    def target(t):
        if t == 0:
            return down_ref, 0
        if t <= rows:
            return mid_ref, t - 1
        return up_ref, t - 1 - rows

    for i in range(rows):
        s, right_at, right_w, left_at, left_w = entries[i]
        goes_right = s >= 0
        at = jnp.where(goes_right, right_at, left_at)
        width = jnp.where(goes_right, right_w, left_w)
        om = jnp.bitwise_and(at, cols - 1)
        window = at // cols

        def units(ref, k):
            return ref[jnp.minimum(2 * window + k, unit_count - 1)]

        def unfold(ref):
            low_lane = jnp.bitwise_and(lane_big, unit - 1)
            even = jnp.where(low_lane >= om, units(ref, 0), units(ref, 2))
            odd = jnp.where(low_lane + unit >= om, units(ref, 1), units(ref, 3))
            lo_ref[...] = jnp.where(lane_big < unit, even, pltpu.roll(odd, unit, 1))
            hi_ref[...] = jnp.where(lane_big < unit, pltpu.roll(even, unit, 1), odd)

        @pl.when(goes_right)
        def _():
            unfold(right_ref)

        @pl.when(jnp.logical_not(goes_right))
        def _():
            unfold(left_ref)

        base = jnp.where(goes_right, s - width, s)
        got_shift = base - at
        cut = jnp.where(goes_right, s, s + cols)
        shifts = [
            (jnp.bitwise_and(got_shift + b - 1, cols - 1), jnp.bitwise_and(s + b - 1, cols - 1))
            for b in range(4)
        ]
        from_got = []
        for b in range(4):
            below = (lane - (b - 1)) < cut
            from_got.append(jnp.where(goes_right, below.astype(jnp.int32), 1 - below.astype(jnp.int32)) != 0)

        def terms(got, home):
            return [
                jnp.where(from_got[b], pltpu.roll(got, shifts[b][0], 1), pltpu.roll(home, shifts[b][1], 1))
                for b in range(4)
            ]

        tail = jnp.where(sub8 == 0, fx_ref[i : i + 1, :], fy_ref[i : i + 1, :])
        fractions = terms(hi_ref[half - PIECE : half, :], tail)
        no_left = (s == -1) | (s == cols - 1)
        no_right = (s == 0) | (s == -cols)
        paired = []
        for b in range(4):
            fx = jnp.broadcast_to(fractions[b][0:1, :], (PIECE, cols))
            fy = jnp.broadcast_to(fractions[b][1:2, :], (PIECE, cols))
            wx = wx_weights(fx)[b]
            if b == 3:
                wx = jnp.where((lane == 0) & no_left, 0.0, wx)
            if b == 0:
                wx = jnp.where((lane == cols - 1) & no_right, 0.0, wx)
            wy = wx_weights(fy)
            paired.append([wx * wy[a] for a in range(4)])

        def add(level, got):
            moved = terms(got, x_ref[i, pl.ds(level, PIECE), :])
            for a in range(4):
                total = moved[0] * paired[0][a]
                for b in range(1, 4):
                    total = total + moved[b] * paired[b][a]
                ref, row = target(i + a)
                if not (a == 3 or i == 0):
                    total = total + ref[row, pl.ds(level, PIECE), :]
                ref[row, pl.ds(level, PIECE), :] = total

        def step(r, carry):
            level = pl.multiple_of(r * PIECE, PIECE)
            add(level, lo_ref[pl.ds(level, PIECE), :])
            add(pl.multiple_of(half + r * PIECE, PIECE), hi_ref[pl.ds(level, PIECE), :])
            return carry

        lax.fori_loop(0, (levels - half) // PIECE, step, 0, unroll=5)
        for level in range(levels - half, half, PIECE):
            add(level, lo_ref[level : level + PIECE, :])

        def add_one(ref_of_unit, place, lane_to, b):
            shift_lo = jnp.bitwise_and(lane_to - place, cols - 1)
            shift_hi = jnp.bitwise_and(lane_to - place - unit, cols - 1)
            tail = pltpu.roll(ref_of_unit(half - PIECE), shift_hi, 1)
            wx = wx_weights(jnp.broadcast_to(tail[0:1, :], (PIECE, cols)))[b]
            wy = wx_weights(jnp.broadcast_to(tail[1:2, :], (PIECE, cols)))
            for a in range(4):
                weight_ref[a] = wx * wy[a]

            def put(level, value):
                for a in range(4):
                    ref, row = target(i + a)
                    old = ref[row, pl.ds(level, PIECE), :]
                    ref[row, pl.ds(level, PIECE), :] = jnp.where(lane == lane_to, old + value * weight_ref[a], old)

            def one(r, carry):
                level = pl.multiple_of(r * PIECE, PIECE)
                value = ref_of_unit(level)
                put(level, pltpu.roll(value, shift_lo, 1))

                @pl.when(level < levels - half)
                def _():
                    put(pl.multiple_of(level + half, PIECE), pltpu.roll(value, shift_hi, 1))

                return carry

            lax.fori_loop(0, half // PIECE, one, 0)

        def in_packed(ref, place):
            u = jnp.minimum(place // unit, unit_count - 1)
            return lambda level: ref[u, pl.ds(level, PIECE), :]

        def in_far(ref):
            return lambda level: ref[pl.ds(level, PIECE), :]

        @pl.when(s == -1)
        def _():
            add_one(in_packed(right_ref, right_at), jnp.bitwise_and(right_at, unit - 1), 0, 3)

        @pl.when(s == cols - 1)
        def _():
            add_one(in_far(far_right_ref), i, 0, 3)

        @pl.when(s == 0)
        def _():
            add_one(in_packed(left_ref, left_at), jnp.bitwise_and(left_at, unit - 1), cols - 1, 0)

        @pl.when(s == -cols)
        def _():
            add_one(in_far(far_left_ref), i, cols - 1, 0)


def vertical_kernel(mid_ref, from_prev_ref, from_next_ref, inverse_ref, coupling_ref, out_ref, matrix_ref):
    rows, tracers, levels, cols = out_ref.shape
    size = inverse_ref.shape[2]
    level_of = lax.broadcasted_iota(jnp.int32, (levels, cols), 0)
    dot = functools.partial(jnp.dot, preferred_element_type=jnp.float32)
    matrix_ref[...] = jnp.zeros(matrix_ref.shape, jnp.float32)
    for i in range(rows):
        matrix_ref[0:size, 0:size] = inverse_ref[i, 0]
        matrix_ref[size:levels, size:levels] = inverse_ref[i, 1]
        matrix = matrix_ref[...]
        m_hi = matrix.astype(jnp.bfloat16)
        m_lo = (matrix - m_hi.astype(jnp.float32)).astype(jnp.bfloat16)
        edge = jnp.where(
            level_of[:, 0:1] < size, matrix[:, size - 1 : size], matrix[:, size : size + 1]
        )
        edge = jnp.broadcast_to(edge, (levels, cols))
        for t in range(tracers):
            field = mid_ref[i, t]
            if i < 2:
                field = field + from_prev_ref[i, t]
            if i == rows - 1:
                field = field + from_next_ref[0, t]
            f_hi = field.astype(jnp.bfloat16)
            f_lo = (field - f_hi.astype(jnp.float32)).astype(jnp.bfloat16)
            first = dot(m_hi, f_hi) + (dot(m_hi, f_lo) + dot(m_lo, f_hi))
            coupling = coupling_ref[i : i + 1, :]
            other = jnp.where(
                level_of < size, coupling * first[size : size + 1, :], coupling * first[size - 1 : size, :]
            )
            out_ref[i, t] = first + edge * other


def on_device(adjoint_in, frac_x, frac_y, dep_tile, dep_col, block_inverse, coupling):
    rows, tracers, levels, cols = adjoint_in.shape
    flat = tracers * levels
    half = (flat + 2 + 2 * PIECE - 1) // (2 * PIECE) * PIECE
    unit_count = 2 * rows
    x = adjoint_in.reshape(rows, flat, cols)
    f32 = jnp.float32
    vmem = pl.BlockSpec(memory_space=pltpu.VMEM)
    smem = pl.BlockSpec(memory_space=pltpu.SMEM)
    params = pltpu.CompilerParams(vmem_limit_bytes=VMEM_BYTES)

    right, left, far_right, far_left, index = pl.pallas_call(
        pack_kernel,
        name="pack",
        out_shape=(
            jax.ShapeDtypeStruct((unit_count, half, cols), f32),
            jax.ShapeDtypeStruct((unit_count, half, cols), f32),
            jax.ShapeDtypeStruct((half, cols), f32),
            jax.ShapeDtypeStruct((half, cols), f32),
            jax.ShapeDtypeStruct((1,), jnp.int32),
        ),
        in_specs=[smem, smem, vmem, vmem, vmem],
        out_specs=(vmem, vmem, vmem, vmem, smem),
        scratch_shapes=[pltpu.VMEM((half, cols), f32), pltpu.VMEM((half, cols), f32)],
        compiler_params=params,
    )(dep_tile, dep_col, x, frac_x, frac_y)

    far_right = passed_along(far_right, "lon", 2)
    far_left = passed_along(far_left, "lon", -2)

    def exchange(right_units, left_units):
        def run(right, left):
            got_right, got_left = right, left
            if right_units:
                got = passed_along(right[:right_units], "lon", 1)
                got_right = lax.dynamic_update_slice(right, got, (0, 0, 0))
            if left_units:
                got = passed_along(left[:left_units], "lon", -1)
                got_left = lax.dynamic_update_slice(left, got, (0, 0, 0))
            return got_right, got_left

        return run

    branches, numbers = [], []
    for r in range(unit_count + 1):
        for l in range(unit_count + 1):
            if r + l <= unit_count + 1:
                numbers.append(len(branches))
                branches.append(exchange(r, l))
            else:
                numbers.append(0)
    r = index[0] // (unit_count + 1)
    l = index[0] % (unit_count + 1)
    starts = [numbers[k * (unit_count + 1)] for k in range(unit_count + 1)]
    which = l
    for k in range(1, unit_count + 1):
        which = which + jnp.where(r >= k, starts[k] - starts[k - 1], 0)
    right, left = lax.switch(which, branches, right, left)

    down, mid, up = pl.pallas_call(
        spread_kernel,
        name="spread",
        out_shape=(
            jax.ShapeDtypeStruct((1, flat, cols), f32),
            jax.ShapeDtypeStruct((rows, flat, cols), f32),
            jax.ShapeDtypeStruct((2, flat, cols), f32),
        ),
        in_specs=[smem, smem, vmem, vmem, vmem, vmem, vmem, vmem, vmem],
        out_specs=(vmem, vmem, vmem),
        scratch_shapes=[
            pltpu.VMEM((half, cols), f32),
            pltpu.VMEM((half, cols), f32),
            pltpu.VMEM((4, PIECE, cols), f32),
        ],
        compiler_params=params,
    )(dep_tile, dep_col, x, frac_x, frac_y, right, left, far_right, far_left)

    from_prev = shifted(up, "lat", 1)
    from_next = shifted(down, "lat", -1)

    return pl.pallas_call(
        vertical_kernel,
        name="vertical",
        out_shape=jax.ShapeDtypeStruct(adjoint_in.shape, f32),
        in_specs=[vmem, vmem, vmem, vmem, vmem],
        out_specs=vmem,
        scratch_shapes=[pltpu.VMEM((levels, levels), f32)],
        compiler_params=params,
    )(
        mid.reshape(rows, tracers, levels, cols),
        from_prev.reshape(2, tracers, levels, cols),
        from_next.reshape(1, tracers, levels, cols),
        block_inverse,
        coupling,
    )


def solution(mesh):
    return jax.shard_map(
        on_device,
        mesh=mesh,
        in_specs=(
            P("lat", None, None, "lon"),
            P("lat", "lon"),
            P("lat", "lon"),
            P("lat"),
            P("lat"),
            P("lat", None, None, None),
            P("lat", "lon"),
        ),
        out_specs=P("lat", None, None, "lon"),
        check_vma=False,
    )
```

time: 230 us -> 49.3 us (0.21)
  loops' own time: 102 us -> 0.5 us
  other arithmetic: 61.2 us -> 0 us
  local copies, waits for them, and re-layouts: 43.8 us -> 4.65 us
  waiting for transfers between devices: 5.16 us -> 15.3 us
  Pallas kernels: 0 us -> 8.78 us
  starting transfers between devices: 13 us -> 17.5 us
    another operation x5 -> x1, loops' own time: 102 us -> 0.5 us  [on_device(): right, left = lax.switch(which, branches, right, left)]
    scatter-add x17 -> x0, other arithmetic: 26.3 us -> none  [the longest x15 26.2 us: tile_terms(): extended = extended.at[a:a + row_count].add(summed[:, a])]
    dynamic_update_slice x20 -> x0, other arithmetic: 22.3 us -> none  [tile_terms(): summed = lax.map(one_row, (padded_values, padded_pairs, offsets))]
    ppermute x4, waiting for transfers between devices: 0.01 us -> 14.3 us  [passed_along(): lax.ppermute(x, axis, [(i, (i + by) % devices) for i in range(devices)])]
    dynamic_slice x20 -> x0, local copies, waits for them, and re-layouts: 12.5 us -> none  [tile_terms(): summed = lax.map(one_row, (padded_values, padded_pairs, offsets))]
    pallas_call x0 -> x3, Pallas kernels: none -> 8.78 us  [the longest x1 4.86 us: on_device(): pl.pallas_call(spread_kernel, name='spread', out_shape=(jax.ShapeDtypeStr...]
    another operation x5 -> x0, local copies, waits for them, and re-layouts: 8.38 us -> none
    add x5 -> x0, local copies, waits for them, and re-layouts: 6.77 us -> none  [tile_terms(): extended = extended.at[a:a + row_count].add(summed[:, a])]
  transfers between devices with their start and end apart: 6 -> 6, of which waited for: 2 -> 3; matrix products, arithmetic and copies ran while one was open for 31% -> 0% of each run, Pallas kernels for 0% -> 0%
where the time goes in v1:
time: 49.3 us; the launch traced here: 48.8 us
  starting transfers between devices  17.5 us (35%)
  waiting for transfers between devices  15.3 us (31%)
  Pallas kernels  8.78 us (18%)
  local copies, waits for them, and re-layouts  4.65 us (9%)
  between operations  2.11 us (4%)
  loops' own time  0.5 us (1%)
    ppermute x4, waiting for transfers between devices, passed_along(): lax.ppermute(x, axis, [(i, (i + by) % devices) for i in range(devices)])  14.3 us
    ppermute x2, starting transfers between devices, shifted(): return lax.ppermute(x, axis, pairs)  8.93 us
    ppermute x4, starting transfers between devices, passed_along(): lax.ppermute(x, axis, [(i, (i + by) % devices) for i in range(devices)])  8.54 us
    pallas_call x1, Pallas kernels, on_device(): pl.pallas_call(spread_kernel, name='spread', out_shape=(jax.ShapeDtypeStr...  4.86 us
    unnamed x21, local copies, waits for them, and re-layouts  4.55 us
    pallas_call x1, Pallas kernels, on_device(): pl.pallas_call(pack_kernel, name='pack', out_shape=(jax.ShapeDtypeStruct(...  2.1 us
    pallas_call x1, Pallas kernels, on_device(): pl.pallas_call(vertical_kernel, name='vertical', out_shape=jax.ShapeDtype...  1.82 us
    ppermute x2, waiting for transfers between devices, shifted(): return lax.ppermute(x, axis, pairs)  1.03 us
  transfers between devices with their start and end apart: 6, of which 3 were waited for; matrix products, arithmetic and copies ran while one was open for 0% of the time, Pallas kernels for 0%

profile of v1, /device:TPU:1, one launch (start us, length us, event | category | flops | bytes accessed | tf_op | source)
XLA Modules:
  0.0 48.8 jit_solution(10860103304574391700)
XLA Ops:
  0.0 0.0 copy-start.6
  0.0 0.0 copy-start.7
  0.0 0.7 %copy-done.6 = s32[4]{0:T(128)S(1)} copy-done((s32[4]{0:T(128)S(1)}, s32[4]{0:T(128)}, u32[]{:S(2)}) %copy-start.6) | copy-done | bytes 40
  0.7 0.0 copy-done.7
  0.7 0.0 copy-start
  0.7 1.1 %copy-done = f32[4,3,136,128]{3,2,1,0:T(8,128)S(1)} copy-done((f32[4,3,136,128]{3,2,1,0:T(8,128)S(1)}, f32[4,3,136,128]{3,2,1,0:T(8,128)}, u32[]{:S(2)}) %copy-start) | copy-done | bytes 835608
  1.8 0.0 copy-start.2
  1.8 0.7 %copy-done.2 = f32[4,128]{1,0:T(4,128)S(1)} copy-done((f32[4,128]{1,0:T(4,128)S(1)}, f32[4,128]{1,0:T(4,128)}, u32[]{:S(2)}) %copy-start.2) | copy-done | bytes 2072
  2.5 0.0 copy-start.4
  2.5 0.7 %copy-done.4 = f32[4,128]{1,0:T(4,128)S(1)} copy-done((f32[4,128]{1,0:T(4,128)S(1)}, f32[4,128]{1,0:T(4,128)}, u32[]{:S(2)}) %copy-start.4) | copy-done | bytes 2072
  3.2 2.1 %pack.1 = (f32[8,208,128]{2,1,0:T(8,128)S(1)}, f32[8,208,128]{2,1,0:T(8,128)S(1)}, f32[208,128]{1,0:T(8,128)S(1)}, f32[208,128]{1,0:T(8,128)S(1)}, s32[1]{0:T(128)}) custom-call(s32[4]{0:T(128)S(1)} %copy-done.6, s32[4]{0:T(128)S(1)} %copy-done.7, f32[4,408,128]{2,1,0:T(8,128)S(1)} %bitcast.7, f32[4,128]{1,0:T(4,128)S(1)} %copy-done.2, f32[4,128]{1,0:T(4,128)S(1)} %copy-done.4), custom_call_target="tpu_custom_call" | custom-call | tf_op jit(solution)/shard_map/pack/pallas_call | solution.py:302
  5.3 2.2 %collective-permute-start.88 = (f32[208,128]{1,0:T(8,128)S(1)}, f32[208,128]{1,0:T(8,128)S(1)}, u32[]{:S(2)}, u32[]{:S(2)}) collective-permute-start(f32[208,128]{1,0:T(8,128)S(1)} %get-tuple-element.336), channel_id=1, source_target_pairs={{0,2},{1,3},{2,4},{3,5},{4,6},{5,7},{6,0},{7,1},{8,10},{9,11},{10,... | collective-permute-start | bytes 319496 | tf_op jit(solution)/shard_map/ppermute | solution.py:16
  7.5 2.1 %collective-permute-start.89 = (f32[208,128]{1,0:T(8,128)S(1)}, f32[208,128]{1,0:T(8,128)S(1)}, u32[]{:S(2)}, u32[]{:S(2)}) collective-permute-start(f32[208,128]{1,0:T(8,128)S(1)} %get-tuple-element.337), channel_id=1, source_target_pairs={{0,6},{1,7},{2,0},{3,1},{4,2},{5,3},{6,4},{7,5},{8,14},{9,15},{10,... | collective-permute-start | bytes 319496 | tf_op jit(solution)/shard_map/ppermute | solution.py:16
  11.6 0.0 copy-start.1
  11.6 19.1 %conditional.1 = ((f32[8,208,128]{2,1,0:T(8,128)S(1)}, f32[8,208,128]{2,1,0:T(8,128)S(1)})) conditional(s32[]{:T(128)} %clamp.3, (f32[8,208,128]{2,1,0:T(8,128)S(1)}, f32[8,208,128]{2,1,0:T(8,128)S(1)}) %tuple.216, (f32[8,208,128]{2,1,0:T(8,128)S(1)}, f32[8,208,128]{2,1,0:T(8,128)S(1)}) %tuple.217, ...), branch_computations={%region_0.1_spmd, %region_1.2_spmd, %region_2.3_spmd, %region_3.4_... | conditional | bytes 7667816 | solution.py:348
  11.7 1.3 %collective-permute-start.48 = (f32[3,208,128]{2,1,0:T(8,128)S(1)}, f32[3,208,128]{2,1,0:T(8,128)S(1)}, u32[]{:S(2)}, u32[]{:S(2)}) collective-permute-start(f32[3,208,128]{2,1,0:T(8,128)S(1)} %slice.213), channel_id=1, source_target_pairs={{0,1},{1,2},{2,3},{3,4},{4,5},{5,6},{6,7},{7,0},{8,9},{9,10},{10,1... | collective-permute-start | bytes 958472 | tf_op jit(solution)/shard_map/cond/branch_30_fun/ppermute | solution.py:16
  13.0 3.0 %collective-permute-start.49 = (f32[4,208,128]{2,1,0:T(8,128)S(1)}, f32[4,208,128]{2,1,0:T(8,128)S(1)}, u32[]{:S(2)}, u32[]{:S(2)}) collective-permute-start(f32[4,208,128]{2,1,0:T(8,128)S(1)} %slice.214), channel_id=1, source_target_pairs={{0,7},{1,0},{2,1},{3,2},{4,3},{5,4},{6,5},{7,6},{8,15},{9,8},{10,9... | collective-permute-start | bytes 1277960 | tf_op jit(solution)/shard_map/cond/branch_30_fun/ppermute | solution.py:16
  16.0 13.4 %collective-permute-done.48 = f32[3,208,128]{2,1,0:T(8,128)S(1)} collective-permute-done((f32[3,208,128]{2,1,0:T(8,128)S(1)}, f32[3,208,128]{2,1,0:T(8,128)S(1)}, u32[]{:S(2)}, u32[]{:S(2)}) %collective-permute-start.48) | collective-permute-done | bytes 319520 | tf_op jit(solution)/shard_map/cond/branch_30_fun/ppermute | solution.py:16
  29.4 0.8 %collective-permute-done.49 = f32[4,208,128]{2,1,0:T(8,128)S(1)} collective-permute-done((f32[4,208,128]{2,1,0:T(8,128)S(1)}, f32[4,208,128]{2,1,0:T(8,128)S(1)}, u32[]{:S(2)}, u32[]{:S(2)}) %collective-permute-start.49) | collective-permute-done | bytes 426016 | tf_op jit(solution)/shard_map/cond/branch_30_fun/ppermute | solution.py:16
  30.7 0.0 copy-start.5
  30.7 0.0 copy-start.3
  30.7 0.0 collective-permute-done.88.far_right_ref
  30.7 0.0 collective-permute-done.89.far_left_ref
  30.8 0.0 copy-done.1
  30.8 0.6 %copy-done.5 = f32[4,128]{1,0:T(4,128)S(1)} copy-done((f32[4,128]{1,0:T(4,128)S(1)}, f32[4,128]{1,0:T(4,128)}, u32[]{:S(2)}) %copy-start.5) | copy-done | bytes 2072
  31.4 0.0 copy-done.3
  31.4 0.0 copy-start.9
  31.4 4.9 %spread.1 = (f32[1,408,128]{2,1,0:T(8,128)S(1)}, f32[4,408,128]{2,1,0:T(8,128)S(1)}, f32[2,408,128]{2,1,0:T(8,128)S(1)}) custom-call(s32[4]{0:T(128)S(1)} %copy-done.6, s32[4]{0:T(128)S(1)} %copy-done.7, f32[4,408,128]{2,1,0:T(8,128)S(1)} %bitcast.8, f32[4,128]{1,0:T(4,128)S(1)} %copy-done.3, f32[4,128]{1,0:T(4,128)S(1)} %copy-done.5, ...), custom_call_target="tpu_custom_call" | custom-call | tf_op jit(solution)/shard_map/spread/pallas_call | solution.py:350
  36.3 1.9 %collective-permute-start.90 = (f32[2,408,128]{2,1,0:T(8,128)S(1)}, f32[2,408,128]{2,1,0:T(8,128)S(1)}, u32[]{:S(2)}, u32[]{:S(2)}) collective-permute-start(f32[2,408,128]{2,1,0:T(8,128)S(1)} %get-tuple-element.339), channel_id=1, source_target_pairs={{0,8},{8,16},{16,24},{1,9},{9,17},{17,25},{2,10},{10,18},{18,26},{... | collective-permute-start | bytes 1253384 | tf_op jit(solution)/shard_map/ppermute | solution.py:22
  38.2 7.0 %collective-permute-start.91 = (f32[1,408,128]{2,1,0:T(8,128)S(1)}, f32[1,408,128]{2,1,0:T(8,128)S(1)}, u32[]{:S(2)}, u32[]{:S(2)}) collective-permute-start(f32[1,408,128]{2,1,0:T(8,128)S(1)} %get-tuple-element.340), channel_id=1, source_target_pairs={{8,0},{16,8},{24,16},{9,1},{17,9},{25,17},{10,2},{18,10},{26,18},{... | collective-permute-start | bytes 626696 | tf_op jit(solution)/shard_map/ppermute | solution.py:22
  45.2 0.0 copy-done.9
  45.3 1.0 %collective-permute-done.91 = f32[1,408,128]{2,1,0:T(8,128)S(1)} collective-permute-done((f32[1,408,128]{2,1,0:T(8,128)S(1)}, f32[1,408,128]{2,1,0:T(8,128)S(1)}, u32[]{:S(2)}, u32[]{:S(2)}) %collective-permute-start.91) | collective-permute-done | bytes 208928 | tf_op jit(solution)/shard_map/ppermute | solution.py:22
  46.3 0.0 collective-permute-done.90
  46.3 0.0 copy-start.8
  46.3 0.7 %copy-done.8 = f32[4,128]{1,0:T(4,128)S(1)} copy-done((f32[4,128]{1,0:T(4,128)S(1)}, f32[4,128]{1,0:T(4,128)}, u32[]{:S(2)}) %copy-start.8) | copy-done | bytes 2072
  47.0 1.8 %vertical.1 = f32[4,3,136,128]{3,2,1,0:T(8,128)} custom-call(f32[4,3,136,128]{3,2,1,0:T(8,128)S(1)} %bitcast.9, f32[2,3,136,128]{3,2,1,0:T(8,128)S(1)} %bitcast.10, f32[1,3,136,128]{3,2,1,0:T(8,128)S(1)} %bitcast.11, f32[4,2,68,68]{3,2,1,0:T(8,128)S(1)} %copy.8.inverse_ref, f32[4,128]{1,0:T(4,128)S(1)} %copy-done.8), custom_call_target="tpu_custom_call" | custom-call | tf_op jit(solution)/shard_map/vertical/pallas_call | solution.py:371
  (5 shorter events, 0.1 us)
Async XLA Ops:
  0.0 0.7 %copy-start.6 = (s32[4]{0:T(128)S(1)}, s32[4]{0:T(128)}, u32[]{:S(2)}) copy-start(s32[4]{0:T(128)} %tile_ref.3) | copy-start | bytes 52
  0.0 0.7 %copy-start.7 = (s32[4]{0:T(128)S(1)}, s32[4]{0:T(128)}, u32[]{:S(2)}) copy-start(s32[4]{0:T(128)} %col_ref.3) | copy-start | bytes 52
  0.7 1.1 %copy-start = (f32[4,3,136,128]{3,2,1,0:T(8,128)S(1)}, f32[4,3,136,128]{3,2,1,0:T(8,128)}, u32[]{:S(2)}) copy-start(f32[4,3,136,128]{3,2,1,0:T(8,128)} %param.60) | copy-start | bytes 2506756
  1.8 0.7 %copy-start.2 = (f32[4,128]{1,0:T(4,128)S(1)}, f32[4,128]{1,0:T(4,128)}, u32[]{:S(2)}) copy-start(f32[4,128]{1,0:T(4,128)} %fx_ref.3) | copy-start | bytes 6148
  2.5 0.7 %copy-start.4 = (f32[4,128]{1,0:T(4,128)S(1)}, f32[4,128]{1,0:T(4,128)}, u32[]{:S(2)}) copy-start(f32[4,128]{1,0:T(4,128)} %fy_ref.3) | copy-start | bytes 6148
  5.3 25.4 %collective-permute-start.88 = (f32[208,128]{1,0:T(8,128)S(1)}, f32[208,128]{1,0:T(8,128)S(1)}, u32[]{:S(2)}, u32[]{:S(2)}) collective-permute-start(f32[208,128]{1,0:T(8,128)S(1)} %get-tuple-element.336), channel_id=1, source_target_pairs={{0,2},{1,3},{2,4},{3,5},{4,6},{5,7},{6,0},{7,1},{8,10},{9,11},{10,... | collective-permute-start | bytes 319496 | tf_op jit(solution)/shard_map/ppermute | solution.py:16
  7.5 23.3 %collective-permute-start.89 = (f32[208,128]{1,0:T(8,128)S(1)}, f32[208,128]{1,0:T(8,128)S(1)}, u32[]{:S(2)}, u32[]{:S(2)}) collective-permute-start(f32[208,128]{1,0:T(8,128)S(1)} %get-tuple-element.337), channel_id=1, source_target_pairs={{0,6},{1,7},{2,0},{3,1},{4,2},{5,3},{6,4},{7,5},{8,14},{9,15},{10,... | collective-permute-start | bytes 319496 | tf_op jit(solution)/shard_map/ppermute | solution.py:16
  11.6 19.2 %copy-start.1 = (f32[4,3,136,128]{3,2,1,0:T(8,128)S(1)}, f32[4,3,136,128]{3,2,1,0:T(8,128)}, u32[]{:S(2)}) copy-start(f32[4,3,136,128]{3,2,1,0:T(8,128)} %param.60) | copy-start | bytes 2506756
  11.7 17.7 %collective-permute-start.48 = (f32[3,208,128]{2,1,0:T(8,128)S(1)}, f32[3,208,128]{2,1,0:T(8,128)S(1)}, u32[]{:S(2)}, u32[]{:S(2)}) collective-permute-start(f32[3,208,128]{2,1,0:T(8,128)S(1)} %slice.213), channel_id=1, source_target_pairs={{0,1},{1,2},{2,3},{3,4},{4,5},{5,6},{6,7},{7,0},{8,9},{9,10},{10,1... | collective-permute-start | bytes 958472 | tf_op jit(solution)/shard_map/cond/branch_30_fun/ppermute | solution.py:16
  13.0 17.3 %collective-permute-start.49 = (f32[4,208,128]{2,1,0:T(8,128)S(1)}, f32[4,208,128]{2,1,0:T(8,128)S(1)}, u32[]{:S(2)}, u32[]{:S(2)}) collective-permute-start(f32[4,208,128]{2,1,0:T(8,128)S(1)} %slice.214), channel_id=1, source_target_pairs={{0,7},{1,0},{2,1},{3,2},{4,3},{5,4},{6,5},{7,6},{8,15},{9,8},{10,9... | collective-permute-start | bytes 1277960 | tf_op jit(solution)/shard_map/cond/branch_30_fun/ppermute | solution.py:16
  30.7 0.7 %copy-start.5 = (f32[4,128]{1,0:T(4,128)S(1)}, f32[4,128]{1,0:T(4,128)}, u32[]{:S(2)}) copy-start(f32[4,128]{1,0:T(4,128)} %fy_ref.3) | copy-start | bytes 6148
  30.7 0.7 %copy-start.3 = (f32[4,128]{1,0:T(4,128)S(1)}, f32[4,128]{1,0:T(4,128)}, u32[]{:S(2)}) copy-start(f32[4,128]{1,0:T(4,128)} %fx_ref.3) | copy-start | bytes 6148
  31.4 13.8 %copy-start.9 = (f32[4,2,68,68]{3,1,2,0:T(2,128)S(1)}, f32[4,2,68,68]{3,1,2,0:T(2,128)}, u32[]{:S(2)}) copy-start(f32[4,2,68,68]{3,1,2,0:T(2,128)} %param.65) | copy-start | bytes 443908
  36.3 10.0 %collective-permute-start.90 = (f32[2,408,128]{2,1,0:T(8,128)S(1)}, f32[2,408,128]{2,1,0:T(8,128)S(1)}, u32[]{:S(2)}, u32[]{:S(2)}) collective-permute-start(f32[2,408,128]{2,1,0:T(8,128)S(1)} %get-tuple-element.339), channel_id=1, source_target_pairs={{0,8},{8,16},{16,24},{1,9},{9,17},{17,25},{2,10},{10,18},{18,26},{... | collective-permute-start | bytes 1253384 | tf_op jit(solution)/shard_map/ppermute | solution.py:22
  38.2 8.1 %collective-permute-start.91 = (f32[1,408,128]{2,1,0:T(8,128)S(1)}, f32[1,408,128]{2,1,0:T(8,128)S(1)}, u32[]{:S(2)}, u32[]{:S(2)}) collective-permute-start(f32[1,408,128]{2,1,0:T(8,128)S(1)} %get-tuple-element.340), channel_id=1, source_target_pairs={{8,0},{16,8},{24,16},{9,1},{17,9},{25,17},{10,2},{18,10},{26,18},{... | collective-permute-start | bytes 626696 | tf_op jit(solution)/shard_map/ppermute | solution.py:22
  46.3 0.7 %copy-start.8 = (f32[4,128]{1,0:T(4,128)S(1)}, f32[4,128]{1,0:T(4,128)}, u32[]{:S(2)}) copy-start(f32[4,128]{1,0:T(4,128)} %coupling_ref.1) | copy-start | bytes 6148
